TPU v7x, 32 devices: a whole 2x2x4 slice. The times are simulated.
32 devices in a mesh: tm: 4 (over x, core), space: 8 (over z, y).
Axes of the slice: x: 2, y: 2, z: 4, core: 2. Of those that a mesh axis runs over, the one named last changes fastest.
Arguments:
- snapshots: bfloat16 [8, 32, 4, 512], P('tm', 'space'), may hold values from -6 to 6
- conv_weight: bfloat16 [32, 4, 3, 3, 3], replicated, may hold values from -0.625 to 0.625
- conv_bias: float32 [32], replicated, may hold values from -3 to 3
- tap_weight: bfloat16 [3, 32, 3, 32], replicated, may hold values from -0.625 to 0.625
- tap_bias: float32 [3, 32], replicated, may hold values from -3 to 3
- mix_weight: bfloat16 [3, 32, 32], replicated, may hold values from -1 to 1
- mix_bias: float32 [3, 32], replicated, may hold values from -3 to 3
Outputs:
- refined: bfloat16 [8, 32, 32, 512], P('tm', 'space')
All inputs are finite; a program needn't handle non-finite values.
Results may differ from a plain program's by a relative error of at most 0.0063.
Values may be sent and summed in bfloat16 or wider, within the bound.
No kernel may reach another device: no remote copies, remote signals or barrier semaphores. Data moves between devices by JAX's collectives and lax.ppermute only.
A program may use at most 64 MiB of HBM per device.

v0:
```python
import jax
import jax.numpy as jnp
from jax import lax
from jax.sharding import PartitionSpec as P

LEVELS = 3
NZ = 32


def with_halo(block, sides, width):
    for axis, dim in sides:
        count = lax.axis_size(axis)
        forward = [(i, i + 1) for i in range(count - 1)]
        forward.append((count - 1, 0))
        backward = [(target, source) for source, target in forward]
        low = lax.ppermute(
            lax.slice_in_dim(block, block.shape[dim] - width, None, axis=dim), axis, forward
        )
        high = lax.ppermute(lax.slice_in_dim(block, 0, width, axis=dim), axis, backward)
        block = jnp.concatenate([low, block, high], axis=dim)
    return block


def spatial_section(padded, conv_flat, conv_shift):
    frame_count, rows_pad, field_count, lines_pad, depth_count = padded.shape
    row_count = rows_pad - 2
    line_count = lines_pad - 2
    walled = jnp.pad(padded, ((0, 0), (0, 0), (0, 0), (0, 0), (1, 1)))
    pieces = []
    for delta_x in range(3):
        for delta_y in range(3):
            for delta_z in range(3):
                pieces.append(
                    walled[
                        :,
                        delta_x : delta_x + row_count,
                        :,
                        delta_y : delta_y + line_count,
                        delta_z : delta_z + depth_count,
                    ]
                )
    patches = jnp.stack(pieces, axis=3).reshape(
        frame_count, row_count, field_count * 27, line_count * depth_count
    )
    summed = jnp.einsum("ok,fxkc->fxoc", conv_flat, patches, preferred_element_type=jnp.float32)
    return jax.nn.gelu(summed + conv_shift[None, None, :, None]).astype(jnp.bfloat16)


def mix_section(current, before, after, tap_flat, tap_shift, mix_flat, mix_shift):
    stacked = jnp.concatenate([before, current, after], axis=2)
    summed = jnp.einsum("ok,txkc->txoc", tap_flat, stacked, preferred_element_type=jnp.float32)
    gated = jax.nn.gelu(summed + tap_shift[None, None, :, None]).astype(jnp.bfloat16)
    mixed = jnp.einsum("ok,txkc->txoc", mix_flat, gated, preferred_element_type=jnp.float32)
    return (current.astype(jnp.float32) + mixed + mix_shift[None, None, :, None]).astype(
        jnp.bfloat16
    )


def local_neighbours(current, spacing):
    blank = jnp.zeros((spacing,) + current.shape[1:], current.dtype)
    before = jnp.concatenate([blank, current[:-spacing]], axis=0)
    after = jnp.concatenate([current[spacing:], blank], axis=0)
    return (before, after)


def shards(snapshots, conv_weight, conv_bias, tap_weight, tap_bias, mix_weight, mix_bias):
    frame_count, row_count, field_count, plane_size = snapshots.shape
    channels = conv_weight.shape[0]
    conv_flat = conv_weight.reshape(channels, field_count * 27)
    tap_flats = tap_weight.reshape(LEVELS, channels, 3 * channels)
    line_count = plane_size // NZ
    margined = with_halo(snapshots, (("space", 1),), 1)
    shaped = margined.reshape(frame_count, row_count + 2, field_count, line_count, NZ)
    wrapped = jnp.concatenate([shaped[:, :, :, -1:], shaped, shaped[:, :, :, :1]], axis=3)
    first = spatial_section(wrapped, conv_flat, conv_bias)
    current = lax.all_to_all(first, "tm", split_axis=3, concat_axis=0, tiled=True)
    for level_index in range(LEVELS):
        before, after = local_neighbours(current, 2**level_index)
        current = mix_section(
            current,
            before,
            after,
            tap_flats[level_index],
            tap_bias[level_index],
            mix_weight[level_index],
            mix_bias[level_index],
        )
    return lax.all_to_all(current, "tm", split_axis=0, concat_axis=3, tiled=True)


def solution(mesh):
    in_specs = (P("tm", "space", None, None), P(), P(), P(), P(), P(), P())
    out_specs = P("tm", "space", None, None)
    return jax.shard_map(shards, mesh=mesh, in_specs=in_specs, out_specs=out_specs, check_vma=False)
```

profile of v0, /device:TPU:0, one launch (start us, length us, event | category | flops | bytes accessed | tf_op | source)
XLA Modules:
  0.0 59.3 jit_solution(7093026501088019217)
XLA Ops:
  0.0 0.7 %fusion.214 = (bf16[2,1,4,512]{3,2,1,0:T(4,128)(2,1)S(1)}, bf16[2,1,4,512]{3,2,1,0:T(4,128)(2,1)S(1)}) fusion(bf16[2,4,4,512]{3,2,1,0:T(4,128)(2,1)} %param.7), kind=kLoop, calls=%fused_computation.226 | loop fusion | bytes 32768 | tf_op jit(solution)/shard_map/slice | solution.py:17
  0.7 3.0 %collective-permute-start = (bf16[2,1,4,512]{3,2,1,0:T(4,128)(2,1)S(1)}, bf16[2,1,4,512]{3,2,1,0:T(4,128)(2,1)S(1)}, u32[]{:S(2)}, u32[]{:S(2)}) collective-permute-start(bf16[2,1,4,512]{3,2,1,0:T(4,128)(2,1)S(1)} %get-tuple-element.16), channel_id=1, source_target_pairs={{0,1},{1,2},{2,3},{3,4},{4,5},{5,6},{6,7},{7,0},{8,9},{9,10},{10,1... | collective-permute-start | bytes 24584 | tf_op jit(solution)/shard_map/ppermute | solution.py:16
  3.7 3.1 %collective-permute-start.1 = (bf16[2,1,4,512]{3,2,1,0:T(4,128)(2,1)S(1)}, bf16[2,1,4,512]{3,2,1,0:T(4,128)(2,1)S(1)}, u32[]{:S(2)}, u32[]{:S(2)}) collective-permute-start(bf16[2,1,4,512]{3,2,1,0:T(4,128)(2,1)S(1)} %get-tuple-element.17), channel_id=1, source_target_pairs={{1,0},{2,1},{3,2},{4,3},{5,4},{6,5},{7,6},{0,7},{9,8},{10,9},{11,1... | collective-permute-start | bytes 24584 | tf_op jit(solution)/shard_map/ppermute | solution.py:19
  6.8 0.8 %fusion.213 = (bf16[1,32,3,32]{3,1,2,0:T(8,128)(2,1)S(1)}, bf16[1,32,3,32]{3,1,2,0:T(8,128)(2,1)S(1)}, bf16[1,32,3,32]{3,1,2,0:T(8,128)(2,1)S(1)}) fusion(bf16[3,32,3,32]{3,1,2,0:T(8,128)(2,1)} %param.10), kind=kLoop, calls=%fused_computation.225 | loop fusion | bytes 36864 | tf_op jit(solution)/shard_map/slice | solution.py:83
  7.6 0.8 %copy.98 = bf16[32,4,3,3,3]{0,4,3,2,1:T(4,128)(2,1)S(1)} copy(bf16[32,4,3,3,3]{0,1,4,3,2:T(4,128)(2,1)} %param.8) | data formatting | bytes 13824 | tf_op args[1]
  8.8 0.8 %pad_maximum_fusion.2 = bf16[2,6,4,512]{3,2,1,0:T(4,128)(2,1)S(1)} fusion(bf16[2,1,4,512]{3,2,1,0:T(4,128)(2,1)S(1)} %collective-permute-done.1, bf16[2,4,4,512]{3,2,1,0:T(4,128)(2,1)} %param.7, bf16[2,1,4,512]{3,2,1,0:T(4,128)(2,1)S(1)} %collective-permute-done), kind=kLoop, calls=%fused_computation.180 | loop fusion | flops 49152 | bytes 98304 | tf_op jit(solution)/shard_map/concatenate | solution.py:20
  9.6 0.2 reshape.23
  9.8 0.3 fusion.107
  10.1 0.7 %fusion.159 = bf16[2,4,4,27,16,32]{5,4,3,2,1,0:T(8,128)(2,1)} fusion(bf16[2,6,4,18,34]{4,3,2,1,0:T(8,128)(2,1)S(1)} %fusion.107), kind=kLoop, calls=%fused_computation.179 | loop fusion | bytes 163840
  10.8 0.7 %fusion.134 = bf16[2,4,4,27,16,32]{5,4,3,2,1,0:T(8,128)(2,1)} fusion(bf16[2,4,4,27,16,32]{5,4,3,2,1,0:T(8,128)(2,1)} %fusion.159, bf16[2,6,4,16,32]{4,3,2,1,0:T(8,128)(2,1)S(1)} %reshape.23, bf16[2,6,4,1,32]{4,3,2,1,0:T(2,128)(2,1)S(1)} %get-tuple-element.11), kind=kLoop, calls=%fused_computation.131 | loop fusion | flops 65536 | bytes 183296
  11.5 0.8 %fusion.158 = bf16[2,4,4,27,16,32]{5,4,3,2,1,0:T(8,128)(2,1)} fusion(bf16[2,4,4,27,16,32]{5,4,3,2,1,0:T(8,128)(2,1)} %fusion.134, bf16[2,6,4,18,34]{4,3,2,1,0:T(8,128)(2,1)S(1)} %fusion.107), kind=kLoop, calls=%fused_computation.177 | loop fusion | bytes 163840
  12.3 0.7 %fusion.157 = bf16[2,4,4,27,16,32]{5,4,3,2,1,0:T(8,128)(2,1)} fusion(bf16[2,4,4,27,16,32]{5,4,3,2,1,0:T(8,128)(2,1)} %fusion.158, bf16[2,6,4,18,34]{4,3,2,1,0:T(8,128)(2,1)S(1)} %fusion.107), kind=kLoop, calls=%fused_computation.175 | loop fusion | bytes 163840
  13.0 0.7 %fusion.156 = bf16[2,4,4,27,16,32]{5,4,3,2,1,0:T(8,128)(2,1)} fusion(bf16[2,4,4,27,16,32]{5,4,3,2,1,0:T(8,128)(2,1)} %fusion.157, bf16[2,6,4,16,32]{4,3,2,1,0:T(8,128)(2,1)S(1)} %reshape.23), kind=kLoop, calls=%fused_computation.173 | loop fusion | bytes 163840
  13.7 0.8 %fusion.155 = bf16[2,4,4,27,16,32]{5,4,3,2,1,0:T(8,128)(2,1)} fusion(bf16[2,4,4,27,16,32]{5,4,3,2,1,0:T(8,128)(2,1)} %fusion.156, bf16[2,6,4,18,34]{4,3,2,1,0:T(8,128)(2,1)S(1)} %fusion.107), kind=kLoop, calls=%fused_computation.171 | loop fusion | bytes 163840
  14.5 0.7 %fusion.154 = bf16[2,4,4,27,16,32]{5,4,3,2,1,0:T(8,128)(2,1)} fusion(bf16[2,4,4,27,16,32]{5,4,3,2,1,0:T(8,128)(2,1)} %fusion.155, bf16[2,6,4,18,34]{4,3,2,1,0:T(8,128)(2,1)S(1)} %fusion.107), kind=kLoop, calls=%fused_computation.169 | loop fusion | bytes 163840
  15.2 0.7 %fusion.128 = bf16[2,4,4,27,16,32]{5,4,3,2,1,0:T(8,128)(2,1)} fusion(bf16[2,4,4,27,16,32]{5,4,3,2,1,0:T(8,128)(2,1)} %fusion.154, bf16[2,6,4,16,32]{4,3,2,1,0:T(8,128)(2,1)S(1)} %reshape.23, bf16[2,6,4,1,32]{4,3,2,1,0:T(2,128)(2,1)S(1)} %get-tuple-element.12), kind=kLoop, calls=%fused_computation.125 | loop fusion | flops 65536 | bytes 183296
  16.0 0.8 %fusion.153 = bf16[2,4,4,27,16,32]{5,4,3,2,1,0:T(8,128)(2,1)} fusion(bf16[2,4,4,27,16,32]{5,4,3,2,1,0:T(8,128)(2,1)} %fusion.128, bf16[2,6,4,18,34]{4,3,2,1,0:T(8,128)(2,1)S(1)} %fusion.107), kind=kLoop, calls=%fused_computation.167 | loop fusion | bytes 163840
  16.8 0.7 %fusion.152 = bf16[2,4,4,27,16,32]{5,4,3,2,1,0:T(8,128)(2,1)} fusion(bf16[2,4,4,27,16,32]{5,4,3,2,1,0:T(8,128)(2,1)} %fusion.153, bf16[2,6,4,18,34]{4,3,2,1,0:T(8,128)(2,1)S(1)} %fusion.107), kind=kLoop, calls=%fused_computation.165 | loop fusion | bytes 163840
  17.5 0.7 %fusion.131 = bf16[2,4,4,27,16,32]{5,4,3,2,1,0:T(8,128)(2,1)} fusion(bf16[2,4,4,27,16,32]{5,4,3,2,1,0:T(8,128)(2,1)} %fusion.152, bf16[2,6,4,16,32]{4,3,2,1,0:T(8,128)(2,1)S(1)} %reshape.23, bf16[2,6,4,1,32]{4,3,2,1,0:T(2,128)(2,1)S(1)} %get-tuple-element.11), kind=kLoop, calls=%fused_computation.128 | loop fusion | flops 65536 | bytes 183296
  18.2 0.8 %fusion.151 = bf16[2,4,4,27,16,32]{5,4,3,2,1,0:T(8,128)(2,1)} fusion(bf16[2,4,4,27,16,32]{5,4,3,2,1,0:T(8,128)(2,1)} %fusion.131, bf16[2,6,4,18,34]{4,3,2,1,0:T(8,128)(2,1)S(1)} %fusion.107), kind=kLoop, calls=%fused_computation.163 | loop fusion | bytes 163840
  19.0 0.7 %fusion.150 = bf16[2,4,4,27,16,32]{5,4,3,2,1,0:T(8,128)(2,1)} fusion(bf16[2,4,4,27,16,32]{5,4,3,2,1,0:T(8,128)(2,1)} %fusion.151, bf16[2,6,4,18,34]{4,3,2,1,0:T(8,128)(2,1)S(1)} %fusion.107), kind=kLoop, calls=%fused_computation.161 | loop fusion | bytes 163840
  19.7 0.7 %fusion.149 = bf16[2,4,4,27,16,32]{5,4,3,2,1,0:T(8,128)(2,1)} fusion(bf16[2,4,4,27,16,32]{5,4,3,2,1,0:T(8,128)(2,1)} %fusion.150, bf16[2,6,4,16,32]{4,3,2,1,0:T(8,128)(2,1)S(1)} %reshape.23), kind=kLoop, calls=%fused_computation.159 | loop fusion | bytes 163840
  20.4 0.8 %fusion.148 = bf16[2,4,4,27,16,32]{5,4,3,2,1,0:T(8,128)(2,1)} fusion(bf16[2,4,4,27,16,32]{5,4,3,2,1,0:T(8,128)(2,1)} %fusion.149, bf16[2,6,4,18,34]{4,3,2,1,0:T(8,128)(2,1)S(1)} %fusion.107), kind=kLoop, calls=%fused_computation.157 | loop fusion | bytes 163840
  21.2 0.7 %fusion.147 = bf16[2,4,4,27,16,32]{5,4,3,2,1,0:T(8,128)(2,1)} fusion(bf16[2,4,4,27,16,32]{5,4,3,2,1,0:T(8,128)(2,1)} %fusion.148, bf16[2,6,4,18,34]{4,3,2,1,0:T(8,128)(2,1)S(1)} %fusion.107), kind=kLoop, calls=%fused_computation.155 | loop fusion | bytes 163840
  21.9 0.7 %fusion.125 = bf16[2,4,4,27,16,32]{5,4,3,2,1,0:T(8,128)(2,1)} fusion(bf16[2,4,4,27,16,32]{5,4,3,2,1,0:T(8,128)(2,1)} %fusion.147, bf16[2,6,4,16,32]{4,3,2,1,0:T(8,128)(2,1)S(1)} %reshape.23, bf16[2,6,4,1,32]{4,3,2,1,0:T(2,128)(2,1)S(1)} %get-tuple-element.12), kind=kLoop, calls=%fused_computation.122 | loop fusion | flops 65536 | bytes 183296
  22.7 0.8 %fusion.146 = bf16[2,4,4,27,16,32]{5,4,3,2,1,0:T(8,128)(2,1)} fusion(bf16[2,4,4,27,16,32]{5,4,3,2,1,0:T(8,128)(2,1)} %fusion.125, bf16[2,6,4,18,34]{4,3,2,1,0:T(8,128)(2,1)S(1)} %fusion.107), kind=kLoop, calls=%fused_computation.153 | loop fusion | bytes 163840
  23.4 0.7 %fusion.145 = bf16[2,4,4,27,16,32]{5,4,3,2,1,0:T(8,128)(2,1)} fusion(bf16[2,4,4,27,16,32]{5,4,3,2,1,0:T(8,128)(2,1)} %fusion.146, bf16[2,6,4,18,34]{4,3,2,1,0:T(8,128)(2,1)S(1)} %fusion.107), kind=kLoop, calls=%fused_computation.151 | loop fusion | bytes 163840
  24.2 0.7 %fusion.144 = bf16[2,4,4,27,16,32]{5,4,3,2,1,0:T(8,128)(2,1)} fusion(bf16[2,4,4,27,16,32]{5,4,3,2,1,0:T(8,128)(2,1)} %fusion.145, bf16[2,6,4,16,32]{4,3,2,1,0:T(8,128)(2,1)S(1)} %reshape.23, bf16[2,6,4,1,32]{4,3,2,1,0:T(2,128)(2,1)S(1)} %get-tuple-element.11), kind=kLoop, calls=%fused_computation.149 | loop fusion | flops 65536 | bytes 183296
  24.9 0.8 %fusion.142 = bf16[2,4,4,27,16,32]{5,4,3,2,1,0:T(8,128)(2,1)} fusion(bf16[2,4,4,27,16,32]{5,4,3,2,1,0:T(8,128)(2,1)} %fusion.144, bf16[2,6,4,18,34]{4,3,2,1,0:T(8,128)(2,1)S(1)} %fusion.107), kind=kLoop, calls=%fused_computation.146 | loop fusion | bytes 163840
  25.7 0.7 %fusion.141 = bf16[2,4,4,27,16,32]{5,4,3,2,1,0:T(8,128)(2,1)} fusion(bf16[2,4,4,27,16,32]{5,4,3,2,1,0:T(8,128)(2,1)} %fusion.142, bf16[2,6,4,18,34]{4,3,2,1,0:T(8,128)(2,1)S(1)} %fusion.107), kind=kLoop, calls=%fused_computation.144 | loop fusion | bytes 163840
  26.4 0.7 %fusion.140 = bf16[2,4,4,27,16,32]{5,4,3,2,1,0:T(8,128)(2,1)} fusion(bf16[2,4,4,27,16,32]{5,4,3,2,1,0:T(8,128)(2,1)} %fusion.141, bf16[2,6,4,16,32]{4,3,2,1,0:T(8,128)(2,1)S(1)} %reshape.23), kind=kLoop, calls=%fused_computation.142 | loop fusion | bytes 163840
  27.1 0.8 %fusion.139 = bf16[2,4,4,27,16,32]{5,4,3,2,1,0:T(8,128)(2,1)} fusion(bf16[2,4,4,27,16,32]{5,4,3,2,1,0:T(8,128)(2,1)} %fusion.140, bf16[2,6,4,18,34]{4,3,2,1,0:T(8,128)(2,1)S(1)} %fusion.107), kind=kLoop, calls=%fused_computation.140 | loop fusion | bytes 163840
  27.9 0.7 %fusion.138 = bf16[2,4,4,27,16,32]{5,4,3,2,1,0:T(8,128)(2,1)} fusion(bf16[2,4,4,27,16,32]{5,4,3,2,1,0:T(8,128)(2,1)} %fusion.139, bf16[2,6,4,18,34]{4,3,2,1,0:T(8,128)(2,1)S(1)} %fusion.107), kind=kLoop, calls=%fused_computation.138 | loop fusion | bytes 163840
  28.6 0.7 %fusion.137 = bf16[2,4,4,27,16,32]{5,4,3,2,1,0:T(8,128)(2,1)} fusion(bf16[2,4,4,27,16,32]{5,4,3,2,1,0:T(8,128)(2,1)} %fusion.138, bf16[2,6,4,1,32]{4,3,2,1,0:T(2,128)(2,1)S(1)} %get-tuple-element.12, bf16[2,6,4,16,32]{4,3,2,1,0:T(8,128)(2,1)S(1)} %reshape.23), kind=kLoop, calls=%fused_computation.136 | loop fusion | flops 65536 | bytes 183296
  29.3 0.8 %fusion.135 = bf16[2,4,4,27,16,32]{5,4,3,2,1,0:T(8,128)(2,1)} fusion(bf16[2,4,4,27,16,32]{5,4,3,2,1,0:T(8,128)(2,1)} %fusion.137, bf16[2,6,4,18,34]{4,3,2,1,0:T(8,128)(2,1)S(1)} %fusion.107), kind=kLoop, calls=%fused_computation.133 | loop fusion | bytes 163840 | tf_op jit(solution)/shard_map/stack | solution.py:42
  30.1 4.9 %reshape.24 = bf16[2,4,108,512]{3,2,1,0:T(8,128)(2,1)S(1)} reshape(bf16[2,4,4,27,16,32]{5,4,3,2,1,0:T(8,128)(2,1)} %fusion.135) | data formatting | bytes 1769472 | tf_op jit(solution)/shard_map/reshape | solution.py:42
  35.1 0.4 fusion.54
  35.5 0.7 %copy.100 = bf16[2,4,32,512]{2,1,0,3:T(4,128)(2,1)S(1)} copy(bf16[2,4,32,512]{3,2,1,0:T(8,128)(2,1)S(1)} %fusion.54) | data formatting | bytes 524288 | tf_op jit(solution)/shard_map/convert_element_type | solution.py:46
  36.2 1.7 %reshape.36 = bf16[4,2,16384]{2,1,0:T(2,128)(2,1)} reshape(bf16[512,2,4,32]{3,2,1,0:T(4,128)(2,1)S(1)} %bitcast.280) | data formatting | bytes 524288
  37.8 3.4 %all-to-all-start = ((bf16[4,2,16384]{2,1,0:T(2,128)(2,1)}), bf16[4,2,16384]{2,1,0:T(2,128)(2,1)S(1)}, u32[]{:S(2)}, u32[]{:S(2)}) async-start(bf16[4,2,16384]{2,1,0:T(2,128)(2,1)} %reshape.36), calls=%async_computation | async-start | bytes 524288 | tf_op jit(solution)/shard_map/all_to_all | solution.py:76
  41.3 6.0 %all-to-all-done = bf16[4,2,16384]{2,1,0:T(2,128)(2,1)S(1)} async-done(((bf16[4,2,16384]{2,1,0:T(2,128)(2,1)}), bf16[4,2,16384]{2,1,0:T(2,128)(2,1)S(1)}, u32[]{:S(2)}, u32[]{:S(2)}) %all-to-all-start) | async-done | bytes 262176 | tf_op jit(solution)/shard_map/all_to_all | solution.py:76
  47.3 0.5 reshape.37
  47.8 0.6 %copy.101 = bf16[2,4,32,4,128]{4,2,1,0,3:T(8,128)(2,1)S(1)} copy(bf16[2,4,32,4,128]{2,1,0,4,3:T(4,128)(2,1)S(1)} %bitcast.281) | data formatting | bytes 524288 | tf_op jit(solution)/shard_map/all_to_all | solution.py:76
  48.5 0.5 fusion.18
  49.1 0.5 fusion.17
  49.6 0.5 fusion.16
  50.2 8.4 %all_to_all.36 = bf16[8,4,32,128]{3,2,1,0:T(8,128)(2,1)S(1)} all-to-all(bf16[8,4,32,128]{3,2,1,0:T(8,128)(2,1)S(1)} %fusion.16), channel_id=1, replica_groups=mesh['tm'=4,'space'=8] {'tm'}, dimensions={0} | all-to-all | bytes 524288 | tf_op jit(solution)/shard_map/all_to_all | solution.py:88
  58.6 0.8 %copy.116 = bf16[4,2,4,4,8,128]{5,4,0,3,2,1:T(8,128)(2,1)} copy(bf16[4,2,4,4,8,128]{5,4,3,2,1,0:T(8,128)(2,1)S(1)} %bitcast.284) | data formatting | bytes 524288 | tf_op jit(solution)/shard_map/all_to_all | solution.py:88
  (22 shorter events, 0.6 us)
Async XLA Ops:
  0.7 8.0 %collective-permute-start = (bf16[2,1,4,512]{3,2,1,0:T(4,128)(2,1)S(1)}, bf16[2,1,4,512]{3,2,1,0:T(4,128)(2,1)S(1)}, u32[]{:S(2)}, u32[]{:S(2)}) collective-permute-start(bf16[2,1,4,512]{3,2,1,0:T(4,128)(2,1)S(1)} %get-tuple-element.16), channel_id=1, source_target_pairs={{0,1},{1,2},{2,3},{3,4},{4,5},{5,6},{6,7},{7,0},{8,9},{9,10},{10,1... | collective-permute-start | bytes 24584 | tf_op jit(solution)/shard_map/ppermute | solution.py:16
  3.7 5.0 %collective-permute-start.1 = (bf16[2,1,4,512]{3,2,1,0:T(4,128)(2,1)S(1)}, bf16[2,1,4,512]{3,2,1,0:T(4,128)(2,1)S(1)}, u32[]{:S(2)}, u32[]{:S(2)}) collective-permute-start(bf16[2,1,4,512]{3,2,1,0:T(4,128)(2,1)S(1)} %get-tuple-element.17), channel_id=1, source_target_pairs={{1,0},{2,1},{3,2},{4,3},{5,4},{6,5},{7,6},{0,7},{9,8},{10,9},{11,1... | collective-permute-start | bytes 24584 | tf_op jit(solution)/shard_map/ppermute | solution.py:19
  23.4 11.6 %copy-start.3 = (f32[32]{0:T(128)S(1)}, f32[32]{0:T(128)}, u32[]{:S(2)}) copy-start(f32[32]{0:T(128)} %param.9) | copy-start | bytes 388
  35.0 6.2 %copy-start = (f32[3,32]{1,0:T(4,128)S(1)}, f32[3,32]{1,0:T(4,128)}, u32[]{:S(2)}) copy-start(f32[3,32]{1,0:T(4,128)} %param.13) | copy-start | bytes 1156
  35.1 6.2 %copy-start.1 = (f32[3,32]{1,0:T(4,128)S(1)}, f32[3,32]{1,0:T(4,128)}, u32[]{:S(2)}) copy-start(f32[3,32]{1,0:T(4,128)} %param.11) | copy-start | bytes 1156
  35.5 13.0 %copy-start.2 = (bf16[3,32,32]{2,1,0:T(8,128)(2,1)S(1)}, bf16[3,32,32]{2,1,0:T(8,128)(2,1)}, u32[]{:S(2)}) copy-start(bf16[3,32,32]{2,1,0:T(8,128)(2,1)} %param.12) | copy-start | bytes 18436
  37.8 9.4 %all-to-all-start = ((bf16[4,2,16384]{2,1,0:T(2,128)(2,1)}), bf16[4,2,16384]{2,1,0:T(2,128)(2,1)S(1)}, u32[]{:S(2)}, u32[]{:S(2)}) async-start(bf16[4,2,16384]{2,1,0:T(2,128)(2,1)} %reshape.36), calls=%async_computation | async-start | bytes 524288 | tf_op jit(solution)/shard_map/all_to_all | solution.py:76
where the time goes:
time: 59.9 us; the launch traced here: 59.3 us
  local copies, waits for them, and re-layouts  27.8 us (46%)
  starting transfers between devices  9.52 us (16%)
  blocking collectives  8.42 us (14%)
  waiting for transfers between devices  5.97 us (10%)
  other arithmetic  5.5 us (9%)
  matrix products  1.93 us (3%)
    unnamed x31, local copies, waits for them, and re-layouts  17.8 us
    all_to_all x1, blocking collectives, shards(): lax.all_to_all(current, 'tm', split_axis=0, concat_axis=3, tiled=True)  8.42 us
    all_to_all x1, waiting for transfers between devices, shards(): lax.all_to_all(first, 'tm', split_axis=3, concat_axis=0, tiled=True)  5.97 us
    reshape x1, local copies, waits for them, and re-layouts, spatial_section(): jnp.stack(pieces, axis=3)  4.92 us
    unnamed x6, other arithmetic  4.4 us
    all_to_all x1, starting transfers between devices, shards(): lax.all_to_all(first, 'tm', split_axis=3, concat_axis=0, tiled=True)  3.41 us
    ppermute x1, starting transfers between devices, with_halo(): lax.ppermute(lax.slice_in_dim(block, 0, width, axis=dim), axis, backward)  3.1 us
    ppermute x1, starting transfers between devices, with_halo(): lax.ppermute(lax.slice_in_dim(block, block.shape[dim] - width, None, axis...  3.01 us
  transfers between devices with their start and end apart: 3, of which 1 were waited for; matrix products, arithmetic and copies ran while one was open for 3% of the time, Pallas kernels for 0%

commit v1 on v0

v1 whole, which is shorter than its diff:
```python
import functools
import math

import jax
import jax.numpy as jnp
from jax import lax
from jax.experimental import pallas as pl
from jax.experimental.pallas import tpu as pltpu
from jax.sharding import PartitionSpec as P

LEVELS = 3
NZ = 32
GROUP = 4
SLOPE = math.sqrt(2.0 / math.pi)
CUBIC = SLOPE * 0.044715
BF16 = jnp.bfloat16
F32 = jnp.float32


def frame_blocks(axis_size, frames):
    needed = [0]
    counts = [1]
    for level in reversed(range(LEVELS)):
        reach = set()
        for offset in needed:
            for frame in range(frames):
                for step in (-(2**level), 2**level):
                    reach.add((offset + (frame + step) // frames) % axis_size)
        needed = needed + sorted(reach - set(needed))
        spare = [offset for offset in range(axis_size) if offset not in needed]
        while len(needed) * frames % GROUP and spare:
            needed.append(spare.pop(0))
        counts.append(len(needed))
    return needed, counts[::-1]


def gelu(value):
    half = 0.5 * value
    return (half + half * jnp.tanh(value * (SLOPE + CUBIC * (value * value)))).astype(BF16)


def column(row, copies):
    count = row.shape[1]
    down = lax.broadcasted_iota(jnp.int32, (count, count), 0)
    across = lax.broadcasted_iota(jnp.int32, (count, count), 1)
    tall = jnp.sum(jnp.where(down == across, row, 0.0), axis=1, keepdims=True)
    return jnp.broadcast_to(jnp.concatenate([tall] * copies, axis=0), (count * copies, 128))


def spread(block, rows, columns):
    channels = block.shape[0]
    tall = jnp.concatenate([block] * (rows // channels), axis=0)
    down = lax.broadcasted_iota(jnp.int32, (channels, columns), 0)
    across = lax.broadcasted_iota(jnp.int32, (channels, columns), 1)
    pick = jnp.where(across % channels == down, 1.0, 0.0).astype(BF16)
    return jnp.dot(tall, pick, preferred_element_type=F32)


def prepare_kernel(slot_of, frames, conv, conv_shift, taps, tap_shift, mix, mix_shift, *outs):
    conv_out, conv_shift_out = outs[0], outs[1]
    tap_outs = outs[2 : 2 + LEVELS]
    tap_shift_out, mix_out, mix_shift_out = outs[2 + LEVELS :]
    channels, depth = conv.shape
    fields = depth // 27
    wide = 27 * GROUP * fields
    down = lax.broadcasted_iota(jnp.int32, (depth, wide), 0)
    across = lax.broadcasted_iota(jnp.int32, (depth, wide), 1)
    same = (down // fields == across // (GROUP * fields)) & (down % fields == across % fields)
    pick = jnp.where(same, 1.0, 0.0).astype(BF16)
    tall = jnp.concatenate([conv[...]] * GROUP, axis=0)
    full = jnp.dot(tall, pick, preferred_element_type=F32)
    down = lax.broadcasted_iota(jnp.int32, full.shape, 0)
    across = lax.broadcasted_iota(jnp.int32, full.shape, 1)
    keep = down // channels == across // fields % GROUP
    conv_out[...] = jnp.where(keep, full, 0.0).astype(BF16)
    conv_shift_out[...] = column(conv_shift[...], GROUP)
    slots = slot_of(lax.axis_index("tm"))
    for level in range(LEVELS):
        rows, columns = tap_outs[level].shape

        def frame_of(axis):
            place = lax.broadcasted_iota(jnp.int32, (rows, columns), axis) // channels
            block = place // frames
            start = jnp.zeros((rows, columns), jnp.int32)
            for index, slot in enumerate(slots[: (rows, columns)[axis] // channels // frames]):
                start = jnp.where(block == index, slot * frames, start)
            return start + place % frames

        gap = frame_of(1) - frame_of(0)
        total = jnp.zeros((rows, columns), F32)
        for tap in range(3):
            block = taps[level, :, tap * channels : (tap + 1) * channels]
            total = jnp.where(
                gap == (tap - 1) * 2**level, spread(block, rows, columns), total
            )
        tap_outs[level][...] = total.astype(BF16)
        tap_shift_out[level] = column(tap_shift[level : level + 1], GROUP)
        size = GROUP * channels
        down = lax.broadcasted_iota(jnp.int32, (size, size), 0)
        across = lax.broadcasted_iota(jnp.int32, (size, size), 1)
        full = spread(mix[level], size, size)
        mix_out[level] = jnp.where(down // channels == across // channels, full, 0.0).astype(BF16)
        mix_shift_out[level] = column(mix_shift[level : level + 1], GROUP)


def shifted(lines):
    plane = lines.shape[-1]
    depth = lax.broadcasted_iota(jnp.int32, (1, plane), 1) % NZ
    blank = jnp.zeros_like(lines)
    below = jnp.where(depth == 0, blank, pltpu.roll(lines, 1, 1))
    above = jnp.where(depth == NZ - 1, blank, pltpu.roll(lines, plane - 1, 1))
    for delta_y in (-1, 0, 1):
        for piece in (below, lines, above):
            yield pltpu.roll(piece, -delta_y * NZ % plane, 1) if delta_y else piece


def wide(shift, plane):
    return jnp.concatenate([shift] * (plane // 128), axis=1)


def encode_kernel(low, own, high, conv, conv_shift, *rest):
    taps = rest[:LEVELS]
    tap_shift, mix, mix_shift, out, patches = rest[LEVELS:]
    row_count, depth, plane = own.shape
    chunk = math.gcd(plane, 512)
    channels = out.shape[2]
    tall = GROUP * channels
    for index in range(row_count + 2):
        if index == 0:
            lines = low[...]
        elif index == row_count + 1:
            lines = high[...]
        else:
            lines = own[index - 1]
        for place, piece in enumerate(shifted(lines)):
            patches[index, place] = piece
    fields = conv.shape[1] // 27
    for row in range(row_count):
        for start in range(0, plane, chunk):
            cells = slice(start, start + chunk)
            parts = []
            for group in range(depth // fields):
                lines = patches[row : row + 3, :, group * fields : (group + 1) * fields, cells]
                summed = jnp.dot(
                    conv[...], lines.reshape(27 * fields, chunk), preferred_element_type=F32
                )
                parts.append(gelu(summed + wide(conv_shift[...], chunk)))
            hidden = jnp.concatenate(parts, axis=0)
            for level, tap in enumerate(taps):
                rows, columns = tap.shape
                summed = jnp.dot(tap[...], hidden[:columns], preferred_element_type=F32)
                parts = []
                for first in range(0, rows, tall):
                    size = min(tall, rows - first)
                    piece = summed[first : first + size]
                    gated = gelu(piece + wide(tap_shift[level, :size], chunk))
                    mixed = jnp.dot(
                        mix[level, :size, :size], gated, preferred_element_type=F32
                    )
                    current = hidden[first : first + size].astype(F32)
                    parts.append(
                        (current + mixed + wide(mix_shift[level, :size], chunk)).astype(BF16)
                    )
                hidden = jnp.concatenate(parts, axis=0)
            for frame in range(out.shape[0]):
                out[frame, row, :, cells] = hidden[frame * channels : (frame + 1) * channels]


VMEM = pl.BlockSpec(memory_space=pltpu.VMEM)
PARAMS = pltpu.CompilerParams(vmem_limit_bytes=40 * 2**20)


def ring(count, step):
    return [(index, (index + step) % count) for index in range(count)]


def shards(snapshots, conv_weight, conv_bias, tap_weight, tap_bias, mix_weight, mix_bias):
    frames, row_count, fields, plane = snapshots.shape
    channels = conv_weight.shape[0]
    times = lax.axis_size("tm")
    spaces = lax.axis_size("space")
    offsets, counts = frame_blocks(times, frames)
    paired = times == 4 and sorted(offsets) == [0, 1, 2, 3]
    tall = GROUP * channels

    if paired:
        offsets = [0, 2, 1, 3]
        across = [(index, index ^ 2) for index in range(times)]
        beside = [(index, index ^ 1) for index in range(times)]
        far = lax.ppermute(snapshots, "tm", across)
        near = lax.ppermute(snapshots, "tm", beside)
        both = lax.ppermute(far, "tm", beside)
        blocks = [snapshots, far, near, both]
        slot_of = lambda index: [index ^ offset for offset in offsets]
    else:
        blocks = [snapshots] + [
            lax.ppermute(snapshots, "tm", ring(times, -offset)) for offset in offsets[1:]
        ]
        slot_of = lambda index: [(index + offset) % times for offset in offsets]

    total = len(blocks) * frames
    rows = jnp.concatenate(blocks, axis=0).transpose(1, 0, 2, 3)
    rows = rows.reshape(row_count, total * fields, plane)

    conv_flat = conv_weight.transpose(0, 2, 3, 4, 1).reshape(channels, 27 * fields)
    tap_flat = tap_weight.reshape(LEVELS, channels, 3 * channels)
    shapes = [
        jax.ShapeDtypeStruct((tall, 27 * GROUP * fields), BF16),
        jax.ShapeDtypeStruct((tall, 128), F32),
    ]
    for level in range(LEVELS):
        shapes.append(
            jax.ShapeDtypeStruct(
                (
                    counts[level + 1] * frames * channels,
                    counts[level] * frames * channels,
                ),
                BF16,
            )
        )
    shapes += [
        jax.ShapeDtypeStruct((LEVELS, tall, 128), F32),
        jax.ShapeDtypeStruct((LEVELS, tall, tall), BF16),
        jax.ShapeDtypeStruct((LEVELS, tall, 128), F32),
    ]
    weights = pl.pallas_call(
        functools.partial(prepare_kernel, slot_of, frames),
        out_shape=shapes,
        in_specs=[VMEM] * 6,
        out_specs=[VMEM] * len(shapes),
        compiler_params=PARAMS,
        name="prepare",
    )(conv_flat, conv_bias.reshape(1, channels), tap_flat, tap_bias, mix_weight, mix_bias)

    if paired:
        core = lax.axis_index("tm") % 2
        message = jnp.where(core == 0, rows[row_count - 1], rows[0])
        pairs = []
        for time in range(times):
            for space in range(spaces):
                target = (space + 1 - 2 * (time % 2)) % spaces
                pairs.append((time * spaces + space, time * spaces + target))
        mine = lax.ppermute(message, ("tm", "space"), pairs)
        other = lax.ppermute(mine, "tm", beside)
        half = total * fields // 2
        other = jnp.concatenate([other[half:], other[:half]], axis=0)
        low = jnp.where(core == 0, mine, other)
        high = jnp.where(core == 0, other, mine)
    else:
        low = lax.ppermute(rows[row_count - 1], "space", ring(spaces, 1))
        high = lax.ppermute(rows[0], "space", ring(spaces, -1))

    return pl.pallas_call(
        encode_kernel,
        out_shape=jax.ShapeDtypeStruct((frames, row_count, channels, plane), BF16),
        in_specs=[VMEM] * (3 + len(weights)),
        out_specs=VMEM,
        scratch_shapes=[pltpu.VMEM((row_count + 2, 9, total * fields, plane), BF16)],
        compiler_params=PARAMS,
        name="encode",
    )(low, rows, high, *weights)


def solution(mesh):
    in_specs = (P("tm", "space", None, None), P(), P(), P(), P(), P(), P())
    out_specs = P("tm", "space", None, None)
    return jax.shard_map(shards, mesh=mesh, in_specs=in_specs, out_specs=out_specs, check_vma=False)
```

time: 59.9 us -> 22.8 us (0.38)
  local copies, waits for them, and re-layouts: 27.8 us -> 1.06 us
  blocking collectives: 8.42 us -> 0 us
  Pallas kernels: 0 us -> 7.14 us
  other arithmetic: 5.5 us -> 0.9 us
  starting transfers between devices: 9.52 us -> 5.05 us
  waiting for transfers between devices: 5.97 us -> 8.24 us
  matrix products: 1.93 us -> 0 us
    unnamed x31 -> x13, local copies, waits for them, and re-layouts: 17.8 us -> 0.74 us
    all_to_all x1 -> x0, blocking collectives: 8.42 us -> none  [shards(): lax.all_to_all(current, 'tm', split_axis=0, concat_axis=3, tiled=True)]
    ppermute x2 -> x5, waiting for transfers between devices: 0.01 us -> 8.24 us  [the longest x1 4.93 us: shards(): mine = lax.ppermute(message, ('tm', 'space'), pairs)]
    pallas_call x0 -> x2, Pallas kernels: none -> 7.14 us  [the longest x1 6.75 us: shards(): pl.pallas_call(encode_kernel, out_shape=jax.ShapeDtypeStruct((frames, row...]
    all_to_all x1 -> x0, waiting for transfers between devices: 5.97 us -> none  [shards(): lax.all_to_all(first, 'tm', split_axis=3, concat_axis=0, tiled=True)]
    reshape x3 -> x4, local copies, waits for them, and re-layouts: 5.1 us -> 0.25 us  [the longest x1 0.11 us: shards(): tap_flat = tap_weight.reshape(LEVELS, channels, 3 * channels)]
    unnamed x6 -> x0, other arithmetic: 4.4 us -> none
    all_to_all x1 -> x0, starting transfers between devices: 3.41 us -> none  [shards(): lax.all_to_all(first, 'tm', split_axis=3, concat_axis=0, tiled=True)]
  transfers between devices with their start and end apart: 3 -> 5, of which waited for: 1 -> 3; matrix products, arithmetic and copies ran while one was open for 3% -> 2% of each run, Pallas kernels for 0% -> 2%
where the time goes in v1:
time: 22.8 us; the launch traced here: 22.5 us
  waiting for transfers between devices  8.24 us (36%)
  Pallas kernels  7.14 us (31%)
  starting transfers between devices  5.05 us (22%)
  local copies, waits for them, and re-layouts  1.06 us (5%)
  other arithmetic  0.9 us (4%)
    pallas_call x1, Pallas kernels, shards(): pl.pallas_call(encode_kernel, out_shape=jax.ShapeDtypeStruct((frames, row...  6.75 us
    ppermute x1, waiting for transfers between devices, shards(): mine = lax.ppermute(message, ('tm', 'space'), pairs)  4.93 us
    ppermute x1, starting transfers between devices, shards(): far = lax.ppermute(snapshots, 'tm', across)  2.94 us
    ppermute x1, starting transfers between devices, shards(): mine = lax.ppermute(message, ('tm', 'space'), pairs)  2.1 us
    ppermute x1, waiting for transfers between devices, shards(): far = lax.ppermute(snapshots, 'tm', across)  2.1 us
    ppermute x1, waiting for transfers between devices, shards(): both = lax.ppermute(far, 'tm', beside)  1.2 us
    transpose x1, other arithmetic, shards(): rows = jnp.concatenate(blocks, axis=0).transpose(1, 0, 2, 3)  0.86 us
    unnamed x13, local copies, waits for them, and re-layouts  0.74 us
  transfers between devices with their start and end apart: 5, of which 3 were waited for; matrix products, arithmetic and copies ran while one was open for 2% of the time, Pallas kernels for 2%

profile of v1, /device:TPU:0, one launch (start us, length us, event | category | flops | bytes accessed | tf_op | source)
XLA Modules:
  0.0 22.5 jit_solution(653979280899263010)
XLA Ops:
  0.0 2.9 %collective-permute-start = (bf16[2,4,4,512]{3,2,1,0:T(4,128)(2,1)}, bf16[2,4,4,512]{3,2,1,0:T(4,128)(2,1)S(1)}, u32[]{:S(2)}, u32[]{:S(2)}) collective-permute-start(bf16[2,4,4,512]{3,2,1,0:T(4,128)(2,1)} %param.7), channel_id=1, source_target_pairs={{0,16},{8,24},{16,0},{24,8},{1,17},{9,25},{17,1},{25,9},{2,18},{10... | collective-permute-start | bytes 98312 | tf_op jit(solution)/shard_map/ppermute | solution.py:190
  2.9 0.0 collective-permute-start.1
  2.9 2.1 %collective-permute-done = bf16[2,4,4,512]{3,2,1,0:T(4,128)(2,1)S(1)} collective-permute-done((bf16[2,4,4,512]{3,2,1,0:T(4,128)(2,1)}, bf16[2,4,4,512]{3,2,1,0:T(4,128)(2,1)S(1)}, u32[]{:S(2)}, u32[]{:S(2)}) %collective-permute-start) | collective-permute-done | bytes 32800 | tf_op jit(solution)/shard_map/ppermute | solution.py:190
  5.0 0.0 collective-permute-start.2
  5.0 0.0 collective-permute-done.1
  5.0 1.2 %collective-permute-done.2 = bf16[2,4,4,512]{3,2,1,0:T(4,128)(2,1)S(1)} collective-permute-done((bf16[2,4,4,512]{3,2,1,0:T(4,128)(2,1)S(1)}, bf16[2,4,4,512]{3,2,1,0:T(4,128)(2,1)S(1)}, u32[]{:S(2)}, u32[]{:S(2)}) %collective-permute-start.2) | collective-permute-done | bytes 32800 | tf_op jit(solution)/shard_map/ppermute | solution.py:192
  6.2 0.9 %maximum_bitcast_fusion = bf16[4,8,4,512]{3,2,0,1:T(4,128)(2,1)S(1)} fusion(bf16[2,4,4,512]{3,2,1,0:T(4,128)(2,1)S(1)} %collective-permute-done.2, bf16[2,4,4,512]{3,2,1,0:T(4,128)(2,1)S(1)} %collective-permute-done.1, bf16[2,4,4,512]{3,2,1,0:T(4,128)(2,1)S(1)} %collective-permute-done, bf16[2,4,4,512]{3,2,1,0:T(4,128)(2,1)} %param.7), kind=kLoop, calls=%fused_computation | loop fusion | flops 196608 | bytes 262144 | tf_op jit(solution)/shard_map/transpose | solution.py:202
  7.1 0.0 copy-start.5
  7.2 0.0 copy-start.4
  7.2 2.1 %collective-permute-start.3 = (bf16[32,512]{1,0:T(8,128)(2,1)S(1)}, bf16[32,512]{1,0:T(8,128)(2,1)S(1)}, u32[]{:S(2)}, u32[]{:S(2)}) collective-permute-start(bf16[32,512]{1,0:T(8,128)(2,1)S(1)} %select_n.32), channel_id=1, source_target_pairs={{0,1},{1,2},{2,3},{3,4},{4,5},{5,6},{6,7},{7,0},{8,15},{9,8},{10,9... | collective-permute-start | bytes 98312 | tf_op jit(solution)/shard_map/ppermute | solution.py:243
  9.3 4.9 %collective-permute-done.3 = bf16[32,512]{1,0:T(8,128)(2,1)S(1)} collective-permute-done((bf16[32,512]{1,0:T(8,128)(2,1)S(1)}, bf16[32,512]{1,0:T(8,128)(2,1)S(1)}, u32[]{:S(2)}, u32[]{:S(2)}) %collective-permute-start.3) | collective-permute-done | bytes 32800 | tf_op jit(solution)/shard_map/ppermute | solution.py:243
  14.2 0.0 collective-permute-start.4
  14.2 0.0 copy-done.5
  14.3 0.1 copy.13.conv
  14.3 0.0 copy-done.4
  14.3 0.1 copy.12
  14.4 0.0 copy-start
  14.4 0.0 copy-start.1
  14.4 0.0 copy-start.2
  14.4 0.1 reshape.21.taps
  14.6 0.0 copy-start.3
  14.6 0.6 %copy-done = bf16[3,32,32]{2,1,0:T(8,128)(2,1)S(1)} copy-done((bf16[3,32,32]{2,1,0:T(8,128)(2,1)S(1)}, bf16[3,32,32]{2,1,0:T(8,128)(2,1)}, u32[]{:S(2)}) %copy-start) | copy-done | bytes 6168
  15.2 0.0 copy-done.1
  15.2 0.0 copy-done.2
  15.2 0.1 copy-done.3
  15.2 0.4 %prepare.1 = (bf16[128,432]{1,0:T(8,128)(2,1)S(1)}, f32[128,128]{1,0:T(8,128)S(1)}, bf16[256,256]{1,0:T(8,128)(2,1)S(1)}, bf16[128,256]{1,0:T(8,128)(2,1)S(1)}, ...) custom-call(bf16[32,108]{1,0:T(8,128)(2,1)S(1)} %copy.13.conv, ...), custom_call_target="tpu_custom_call" | custom-call | tf_op jit(solution)/shard_map/prepare/pallas_call | solution.py:226
  15.7 0.0 collective-permute-done.4
  15.8 6.8 %encode.1 = bf16[2,4,32,512]{3,2,1,0:T(8,128)(2,1)} custom-call(bf16[32,512]{1,0:T(8,128)(2,1)S(1)} %get-tuple-element.22.low, bf16[4,32,512]{2,1,0:T(8,128)(2,1)S(1)} %reshape.18.own, bf16[32,512]{1,0:T(8,128)(2,1)S(1)} %get-tuple-element.21.high, bf16[128,432]{1,0:T(8,128)(2,1)S(1)} %get-tuple-element.13.conv, ...), custom_call_target="tpu_custom_call" | custom-call | tf_op jit(solution)/shard_map/encode/pallas_call | solution.py:253
  (7 shorter events, 0.2 us)
Async XLA Ops:
  0.0 5.0 %collective-permute-start = (bf16[2,4,4,512]{3,2,1,0:T(4,128)(2,1)}, bf16[2,4,4,512]{3,2,1,0:T(4,128)(2,1)S(1)}, u32[]{:S(2)}, u32[]{:S(2)}) collective-permute-start(bf16[2,4,4,512]{3,2,1,0:T(4,128)(2,1)} %param.7), channel_id=1, source_target_pairs={{0,16},{8,24},{16,0},{24,8},{1,17},{9,25},{17,1},{25,9},{2,18},{10... | collective-permute-start | bytes 98312 | tf_op jit(solution)/shard_map/ppermute | solution.py:190
  2.9 2.1 %collective-permute-start.1 = (bf16[2,4,4,512]{3,2,1,0:T(4,128)(2,1)}, bf16[2,4,4,512]{3,2,1,0:T(4,128)(2,1)S(1)}, u32[]{:S(2)}, u32[]{:S(2)}) collective-permute-start(bf16[2,4,4,512]{3,2,1,0:T(4,128)(2,1)} %param.7), channel_id=1, source_target_pairs={{0,8},{8,0},{16,24},{24,16},{1,9},{9,1},{17,25},{25,17},{2,10},{10... | collective-permute-start | bytes 98312 | tf_op jit(solution)/shard_map/ppermute | solution.py:191
  5.0 1.2 %collective-permute-start.2 = (bf16[2,4,4,512]{3,2,1,0:T(4,128)(2,1)S(1)}, bf16[2,4,4,512]{3,2,1,0:T(4,128)(2,1)S(1)}, u32[]{:S(2)}, u32[]{:S(2)}) collective-permute-start(bf16[2,4,4,512]{3,2,1,0:T(4,128)(2,1)S(1)} %collective-permute-done), channel_id=1, source_target_pairs={{0,8},{8,0},{16,24},{24,16},{1,9},{9,1},{17,25},{25,17},{2,10},{10... | collective-permute-start | bytes 98312 | tf_op jit(solution)/shard_map/ppermute | solution.py:192
  7.1 7.1 %copy-start.5 = (bf16[32,4,3,3,3]{0,1,4,3,2:T(4,128)(2,1)S(1)}, bf16[32,4,3,3,3]{0,1,4,3,2:T(4,128)(2,1)}, u32[]{:S(2)}) copy-start(bf16[32,4,3,3,3]{0,1,4,3,2:T(4,128)(2,1)} %param.8) | copy-start | bytes 20740
  7.2 7.2 %copy-start.4 = (bf16[3,32,3,32]{3,1,2,0:T(8,128)(2,1)S(1)}, bf16[3,32,3,32]{3,1,2,0:T(8,128)(2,1)}, u32[]{:S(2)}) copy-start(bf16[3,32,3,32]{3,1,2,0:T(8,128)(2,1)} %param.10) | copy-start | bytes 55300
  7.2 7.0 %collective-permute-start.3 = (bf16[32,512]{1,0:T(8,128)(2,1)S(1)}, bf16[32,512]{1,0:T(8,128)(2,1)S(1)}, u32[]{:S(2)}, u32[]{:S(2)}) collective-permute-start(bf16[32,512]{1,0:T(8,128)(2,1)S(1)} %select_n.32), channel_id=1, source_target_pairs={{0,1},{1,2},{2,3},{3,4},{4,5},{5,6},{6,7},{7,0},{8,15},{9,8},{10,9... | collective-permute-start | bytes 98312 | tf_op jit(solution)/shard_map/ppermute | solution.py:243
  14.2 1.5 %collective-permute-start.4 = (bf16[32,512]{1,0:T(8,128)(2,1)S(1)}, bf16[32,512]{1,0:T(8,128)(2,1)S(1)}, u32[]{:S(2)}, u32[]{:S(2)}) collective-permute-start(bf16[32,512]{1,0:T(8,128)(2,1)S(1)} %collective-permute-done.3), channel_id=1, source_target_pairs={{0,8},{8,0},{16,24},{24,16},{1,9},{9,1},{17,25},{25,17},{2,10},{10... | collective-permute-start | bytes 98312 | tf_op jit(solution)/shard_map/ppermute | solution.py:244
  14.4 0.7 %copy-start = (bf16[3,32,32]{2,1,0:T(8,128)(2,1)S(1)}, bf16[3,32,32]{2,1,0:T(8,128)(2,1)}, u32[]{:S(2)}) copy-start(bf16[3,32,32]{2,1,0:T(8,128)(2,1)} %mix.1) | copy-start | bytes 18436
  14.4 0.7 %copy-start.1 = (f32[3,32]{1,0:T(4,128)S(1)}, f32[3,32]{1,0:T(4,128)}, u32[]{:S(2)}) copy-start(f32[3,32]{1,0:T(4,128)} %tap_shift.1) | copy-start | bytes 1156
  14.4 0.7 %copy-start.2 = (f32[3,32]{1,0:T(4,128)S(1)}, f32[3,32]{1,0:T(4,128)}, u32[]{:S(2)}) copy-start(f32[3,32]{1,0:T(4,128)} %mix_shift.1) | copy-start | bytes 1156
  14.6 0.7 %copy-start.3 = (f32[32]{0:T(128)S(1)}, f32[32]{0:T(128)}, u32[]{:S(2)}) copy-start(f32[32]{0:T(128)} %param.9) | copy-start | bytes 388
